TPU v7x, 512 devices: a whole 4x4x16 slice. The times are simulated.
512 devices in a mesh: vintage: 2 (over core), freq: 4 (over x), tile: 64 (over z, y).
Axes of the slice: x: 4, y: 4, z: 16, core: 2. Of those that a mesh axis runs over, the one named last changes fastest.
Arguments:
- observed: bfloat16 [2, 64, 8, 512, 1024], P('vintage', 'tile', 'freq'), parts along dimension 2, may hold values from -6 to 6
- common_left: bfloat16 [1024, 64, 256], P('freq', 'tile'), parts along dimension 0, may hold values from -1.1953125 to 1.1953125
- common_right: bfloat16 [1024, 64, 256], P('freq', 'tile'), parts along dimension 0, may hold values from -1.1953125 to 1.1953125
- innov_left: bfloat16 [2, 1024, 64, 256], P('vintage', 'freq', 'tile'), parts along dimension 1, may hold values from -0.8984375 to 0.8984375
- innov_right: bfloat16 [2, 1024, 64, 256], P('vintage', 'freq', 'tile'), parts along dimension 1, may hold values from -0.8984375 to 0.8984375
- tile_block_pairs: int32 [2, 64, 8, 2], P(None, None, 'freq'), parts along dimension 2, may hold values from 0 to 31
- live: int32 [2, 64, 8], P(None, None, 'freq'), parts along dimension 2, may hold values from 0 to 1, as said below
- row_mask: int32 [2, 64, 8, 512], P('vintage', 'tile', 'freq'), parts along dimension 2, may hold values 0 or 1
- col_mask: int32 [2, 64, 8, 512], P('vintage', 'tile', 'freq'), parts along dimension 2, may hold values 0 or 1
Outputs:
- new_common_left: float32 [1024, 64, 256], P('freq', 'tile'), parts along dimension 0
- new_common_right: float32 [1024, 64, 256], P('freq', 'tile'), parts along dimension 0
- new_innov_left: float32 [2, 1024, 64, 256], P('vintage', 'freq', 'tile'), parts along dimension 1
- new_innov_right: float32 [2, 1024, 64, 256], P('vintage', 'freq', 'tile'), parts along dimension 1
There are 4 independent parts, one for each index of `freq`. A program takes and returns all parts, laid end to end along the dimension named above; each array names one. Nothing has to cross between parts.
Inputs may be any that keep to these rules, and one draw needn't show every extreme that they name: Each device holds 1 to 2 live slots, the live ones first; in each vintage some device has all 2 live.
All inputs are finite; a program needn't handle non-finite values. No bound on the sum of `row_mask` or of `col_mask` on one device may be relied on, other than what follows from the above.
Results may differ from a plain program's by a relative error of at most 0.0041.
Values may be sent and summed in bfloat16 or wider, within the bound.
A program may use at most 64 MiB of HBM per device.

v0:
```python
import jax
import jax.numpy as jnp
from jax import lax
from jax.sharding import PartitionSpec as P

step_size = 8.0
shrink = 0.5


def tile_terms(
    left_factor_block,
    right_factor_block,
    observed_tile_values,
    row_retained,
    column_retained,
    active_flag,
):
    half = left_factor_block.shape[1] // 2
    tile_len = left_factor_block.shape[0]
    s_real = jnp.concatenate([right_factor_block[:, :half], -right_factor_block[:, half:]], axis=1)
    s_imag = jnp.concatenate([right_factor_block[:, half:], right_factor_block[:, :half]], axis=1)
    stacked = jnp.concatenate([s_real, s_imag], axis=0)
    predicted = lax.dot_general(
        left_factor_block, stacked, (((1,), (1,)), ((), ())), preferred_element_type=jnp.float32
    )
    weight = (
        row_retained.astype(jnp.float32)[:, None]
        * column_retained.astype(jnp.float32)[None, :]
        * active_flag.astype(jnp.float32)
    )
    weight = jnp.concatenate([weight, weight], axis=1)
    misfit = (weight * (predicted - observed_tile_values.astype(jnp.float32))).astype(jnp.bfloat16)
    scale = 1.0 / tile_len
    left_gradient_delta = (
        jnp.dot(misfit, stacked, preferred_element_type=jnp.float32) * scale
    ).astype(jnp.bfloat16)
    cross = lax.dot_general(
        misfit, left_factor_block, (((0,), (0,)), ((), ())), preferred_element_type=jnp.float32
    )
    first = cross[:tile_len]
    second = cross[tile_len:]
    right_gradient_delta = jnp.concatenate(
        [first[:, :half] + second[:, half:], second[:, :half] - first[:, half:]], axis=1
    )
    right_gradient_delta = (right_gradient_delta * scale).astype(jnp.bfloat16)
    return (left_gradient_delta, right_gradient_delta)


def block_sum(received, block_ids, nblocks, rows_dev, factor_width):
    onehot = (block_ids[None, :, :] == jnp.arange(nblocks, dtype=jnp.int32)[:, None, None]).astype(
        jnp.bfloat16
    )
    summed = jnp.einsum("bts,sjtc->bjc", onehot, received, preferred_element_type=jnp.float32)
    return summed.reshape(rows_dev, factor_width)


def per_device(
    observed,
    common_left,
    common_right,
    innov_left,
    innov_right,
    tile_block_pairs,
    live,
    row_mask,
    col_mask,
):
    tile_count_total = lax.axis_size("tile")
    vintage_number = lax.axis_index("vintage")
    device_position = lax.axis_index("tile")
    rows_dev = common_left.shape[0]
    factor_width = common_left.shape[2]
    slots = observed.shape[2]
    tile_len = observed.shape[3]
    per_block = tile_len // tile_count_total
    nblocks = rows_dev // per_block

    def own_blocks(common, innov):
        joined = (common[:, 0].astype(jnp.float32) + innov[0, :, 0].astype(jnp.float32)).astype(
            jnp.bfloat16
        )
        return joined.reshape(nblocks, per_block, factor_width)

    own_left = own_blocks(common_left, innov_left)
    own_right = own_blocks(common_right, innov_right)
    row_indices = lax.dynamic_index_in_dim(
        tile_block_pairs[..., 0], vintage_number, 0, keepdims=False
    )
    column_indices = lax.dynamic_index_in_dim(
        tile_block_pairs[..., 1], vintage_number, 0, keepdims=False
    )
    outgoing = jnp.stack([own_left[row_indices.T], own_right[column_indices.T]], axis=1)[
        :, :, :, :, None, :
    ]
    arrived = lax.all_to_all(outgoing, "tile", split_axis=2, concat_axis=4, tiled=True).reshape(
        slots, 2, tile_len, factor_width
    )
    active_flag = lax.dynamic_index_in_dim(
        lax.dynamic_index_in_dim(live, vintage_number, 0, keepdims=False),
        device_position,
        0,
        keepdims=False,
    )
    left_gradient_delta, right_gradient_delta = jax.vmap(tile_terms)(
        arrived[:, 0], arrived[:, 1], observed[0, 0], row_mask[0, 0], col_mask[0, 0], active_flag
    )
    going_back = jnp.stack([left_gradient_delta, right_gradient_delta], axis=1).reshape(
        slots, 2, per_block, tile_count_total, factor_width
    )
    doubled = jnp.concatenate([going_back, going_back], axis=3)
    returned_block = lax.all_to_all(
        doubled, ("vintage", "tile"), split_axis=3, concat_axis=3, tiled=True
    )
    every_row = tile_block_pairs[..., 0].reshape(2 * tile_count_total, slots)
    every_col = tile_block_pairs[..., 1].reshape(2 * tile_count_total, slots)
    total_left = block_sum(returned_block[:, 0], every_row, nblocks, rows_dev, factor_width)
    total_right = block_sum(returned_block[:, 1], every_col, nblocks, rows_dev, factor_width)
    local_device_slots = lax.dynamic_slice_in_dim(
        returned_block, vintage_number * tile_count_total, tile_count_total, 3
    )
    own_left_grad = block_sum(
        local_device_slots[:, 0], row_indices, nblocks, rows_dev, factor_width
    )
    own_right_grad = block_sum(
        local_device_slots[:, 1], column_indices, nblocks, rows_dev, factor_width
    )

    def update(common, innov, total, own):
        innov_f = innov.astype(jnp.float32)
        new_common = common.astype(jnp.float32) - step_size * total.reshape(
            rows_dev, 1, factor_width
        )
        new_innov = innov_f - step_size * (
            own.reshape(1, rows_dev, 1, factor_width) + shrink * innov_f
        )
        return (new_common, new_innov)

    new_common_left, new_innov_left = update(common_left, innov_left, total_left, own_left_grad)
    new_common_right, new_innov_right = update(
        common_right, innov_right, total_right, own_right_grad
    )
    return (new_common_left, new_common_right, new_innov_left, new_innov_right)


def solution(mesh):
    placed = (
        P("vintage", "tile", "freq", None, None),
        P("freq", "tile", None),
        P("freq", "tile", None),
        P("vintage", "freq", "tile", None),
        P("vintage", "freq", "tile", None),
        P(None, None, "freq", None),
        P(None, None, "freq"),
        P("vintage", "tile", "freq", None),
        P("vintage", "tile", "freq", None),
    )
    return jax.shard_map(
        per_device,
        mesh=mesh,
        in_specs=placed,
        out_specs=(
            P("freq", "tile", None),
            P("freq", "tile", None),
            P("vintage", "freq", "tile", None),
            P("vintage", "freq", "tile", None),
        ),
        check_vma=False,
    )
```

profile of v0, /device:TPU:1, one launch (start us, length us, event | category | flops | bytes accessed | tf_op | source)
XLA Modules:
  0.0 209.2 jit_solution(4010882865037134303)
XLA Ops:
  0.6 0.8 fusion.31
  1.4 0.1 reshape.140
  1.5 0.1 reshape.132
  1.6 1.0 fusion.7
  2.6 1.0 fusion.9
  3.6 0.6 gather_fusion.1
  4.3 0.6 gather_fusion
  4.9 0.1 maximum_bitcast_fusion
  5.0 0.0 copy-start.6
  5.0 0.0 copy-start.4
  5.1 0.0 copy-start.5
  5.1 1.1 copy.37
  6.2 19.3 %all-to-all-start = ((bf16[2,2,64,8,1,256]{5,3,0,1,4,2:T(8,128)(2,1)}), bf16[2,2,64,8,1,256]{5,3,0,1,4,2:T(8,128)(2,1)S(1)}, u32[]{:S(2)}, u32[]{:S(2)}) async-start(bf16[2,2,64,8,1,256]{5,3,0,1,4,2:T(8,128)(2,1)} %copy.37), calls=%async_computation | async-start | bytes 2097152 | tf_op jit(solution)/shard_map/all_to_all | solution.py:95
  25.5 0.0 copy-done.6
  25.5 0.2 fusion.27
  25.7 0.0 copy-done.4
  25.7 0.0 copy-done.5
  25.7 0.2 multiply_multiply_fusion
  26.0 51.0 %all-to-all-done = bf16[2,2,64,8,1,256]{5,3,0,1,4,2:T(8,128)(2,1)S(1)} async-done(((bf16[2,2,64,8,1,256]{5,3,0,1,4,2:T(8,128)(2,1)}), bf16[2,2,64,8,1,256]{5,3,0,1,4,2:T(8,128)(2,1)S(1)}, u32[]{:S(2)}, u32[]{:S(2)}) %all-to-all-start) | async-done | bytes 1048608 | tf_op jit(solution)/shard_map/all_to_all | solution.py:95
  76.9 0.0 copy-start.7
  76.9 0.6 copy.38
  77.5 0.1 slice_negate_fusion
  77.6 0.9 copy-done.7
  78.5 1.0 fusion
  79.5 0.7 fusion.1
  80.3 0.9 fusion.5
  81.2 0.1 slice_add_fusion
  81.3 0.4 copy.40
  81.7 0.4 copy.41
  82.1 0.5 copy.42
  82.7 0.5 fusion.4
  83.2 3.9 %maximum_maximum_fusion = bf16[2,2,8,128,256]{4,0,2,1,3:T(2,128)(2,1)} fusion(bf16[2,1,8,64,256]{4,0,2,1,3:T(2,128)(2,1)S(1)} %fusion.4, bf16[2,1,8,64,256]{4,0,2,1,3:T(2,128)(2,1)S(1)} %copy.42), kind=kLoop, calls=%fused_computation.5 | loop fusion | flops 3145728 | bytes 3145728 | tf_op jit(solution)/shard_map/concatenate | solution.py:110
  87.2 11.3 %all-to-all-start.1 = ((bf16[2,2,8,128,256]{4,0,2,1,3:T(2,128)(2,1)}), bf16[2,2,8,128,256]{4,0,2,1,3:T(2,128)(2,1)S(1)}, u32[]{:S(2)}, u32[]{:S(2)}) async-start(bf16[2,2,8,128,256]{4,0,2,1,3:T(2,128)(2,1)} %maximum_maximum_fusion), calls=%async_computation.1 | async-start | bytes 4194304 | tf_op jit(solution)/shard_map/all_to_all | solution.py:111
  98.5 0.0 copy-start
  98.5 0.1 eq.56
  98.6 0.1 eq.60
  98.7 101.0 %all-to-all-done.1 = bf16[2,2,8,128,256]{4,0,2,1,3:T(2,128)(2,1)S(1)} async-done(((bf16[2,2,8,128,256]{4,0,2,1,3:T(2,128)(2,1)}), bf16[2,2,8,128,256]{4,0,2,1,3:T(2,128)(2,1)S(1)}, u32[]{:S(2)}, u32[]{:S(2)}) %all-to-all-start.1) | async-done | bytes 2097184 | tf_op jit(solution)/shard_map/all_to_all | solution.py:111
  199.7 0.9 constant_dynamic-slice_fusion.1
  200.6 0.3 convolution_bitcast_fusion
  200.9 0.0 copy-done
  200.9 0.2 convert_subtract_fusion.1
  201.1 1.0 copy.54
  202.1 0.0 copy-start.1
  202.1 1.9 fusion.30
  204.0 0.0 copy-start.2
  204.0 0.7 fusion.2
  204.7 0.0 copy-done.1
  204.7 0.0 copy-start.3
  204.7 0.2 convert_subtract_fusion.3
  204.9 1.0 copy.52
  205.9 0.7 fusion.3
  206.6 0.0 copy-done.2
  206.6 0.2 convert_subtract_fusion.4
  206.7 1.0 copy.51
  207.7 0.3 convolution_bitcast_fusion.1
  208.0 0.0 copy-done.3
  208.0 0.2 convert_subtract_fusion.2
  208.2 1.0 copy.53
  (9 shorter events, 0.1 us)
Async XLA Ops:
  5.0 20.5 %copy-start.6 = (s32[2,64,2]{1,2,0:T(2,128)S(1)}, s32[2,64,2]{1,2,0:T(2,128)}, u32[]{:S(2)}) copy-start(s32[2,64,2]{1,2,0:T(2,128)} %param.15) | copy-start | bytes 3076
  5.0 20.6 %copy-start.4 = (s32[1,1,2,512]{3,2,1,0:T(2,128)S(1)}, s32[1,1,2,512]{3,2,1,0:T(2,128)}, u32[]{:S(2)}) copy-start(s32[1,1,2,512]{3,2,1,0:T(2,128)} %param.17) | copy-start | bytes 12292
  5.1 20.6 %copy-start.5 = (s32[1,1,2,512]{3,2,1,0:T(2,128)S(1)}, s32[1,1,2,512]{3,2,1,0:T(2,128)}, u32[]{:S(2)}) copy-start(s32[1,1,2,512]{3,2,1,0:T(2,128)} %param.16) | copy-start | bytes 12292
  6.2 70.7 %all-to-all-start = ((bf16[2,2,64,8,1,256]{5,3,0,1,4,2:T(8,128)(2,1)}), bf16[2,2,64,8,1,256]{5,3,0,1,4,2:T(8,128)(2,1)S(1)}, u32[]{:S(2)}, u32[]{:S(2)}) async-start(bf16[2,2,64,8,1,256]{5,3,0,1,4,2:T(8,128)(2,1)} %copy.37), calls=%async_computation | async-start | bytes 2097152 | tf_op jit(solution)/shard_map/all_to_all | solution.py:95
  76.9 1.6 copy-start.7
  87.2 112.5 %all-to-all-start.1 = ((bf16[2,2,8,128,256]{4,0,2,1,3:T(2,128)(2,1)}), bf16[2,2,8,128,256]{4,0,2,1,3:T(2,128)(2,1)S(1)}, u32[]{:S(2)}, u32[]{:S(2)}) async-start(bf16[2,2,8,128,256]{4,0,2,1,3:T(2,128)(2,1)} %maximum_maximum_fusion), calls=%async_computation.1 | async-start | bytes 4194304 | tf_op jit(solution)/shard_map/all_to_all | solution.py:111
  98.5 102.4 %copy-start = (bf16[1,256,1,256]{3,1,2,0:T(8,128)(2,1)S(1)}, bf16[1,256,1,256]{3,1,2,0:T(8,128)(2,1)}, u32[]{:S(2)}) copy-start(bf16[1,256,1,256]{3,1,2,0:T(8,128)(2,1)} %param.13) | copy-start | bytes 393220
  202.1 2.6 %copy-start.1 = (bf16[256,1,256]{2,0,1:T(8,128)(2,1)S(1)}, bf16[256,1,256]{2,0,1:T(8,128)(2,1)}, u32[]{:S(2)}) copy-start(bf16[256,1,256]{2,0,1:T(8,128)(2,1)} %param.11) | copy-start | bytes 393220
  204.0 2.5 %copy-start.2 = (bf16[256,1,256]{2,0,1:T(8,128)(2,1)S(1)}, bf16[256,1,256]{2,0,1:T(8,128)(2,1)}, u32[]{:S(2)}) copy-start(bf16[256,1,256]{2,0,1:T(8,128)(2,1)} %param.10) | copy-start | bytes 393220
  204.7 3.3 %copy-start.3 = (bf16[1,256,1,256]{3,1,2,0:T(8,128)(2,1)S(1)}, bf16[1,256,1,256]{3,1,2,0:T(8,128)(2,1)}, u32[]{:S(2)}) copy-start(bf16[1,256,1,256]{3,1,2,0:T(8,128)(2,1)} %param.12) | copy-start | bytes 393220
where the time goes:
time: 210 us; the launch traced here: 209 us
  waiting for transfers between devices  152 us (72%)
  starting transfers between devices  30.6 us (15%)
  local copies, waits for them, and re-layouts  13.2 us (6%)
  other arithmetic  7.9 us (4%)
  matrix products  4.61 us (2%)
    all_to_all x1, waiting for transfers between devices, per_device(): lax.all_to_all(doubled, ('vintage', 'tile'), split_axis=3, concat_axis=3,...  101 us
    all_to_all x1, waiting for transfers between devices, per_device(): lax.all_to_all(outgoing, 'tile', split_axis=2, concat_axis=4, tiled=True)  51 us
    all_to_all x1, starting transfers between devices, per_device(): lax.all_to_all(outgoing, 'tile', split_axis=2, concat_axis=4, tiled=True)  19.3 us
    all_to_all x1, starting transfers between devices, per_device(): lax.all_to_all(doubled, ('vintage', 'tile'), split_axis=3, concat_axis=3,...  11.3 us
    unnamed x20, local copies, waits for them, and re-layouts  4.82 us
  transfers between devices with their start and end apart: 2, of which 2 were waited for; matrix products, arithmetic and copies ran while one was open for 0% of the time, Pallas kernels for 0%

commit v1 on v0

v1 whole, which is shorter than its diff:
```python
import jax
import jax.numpy as jnp
from jax import lax
from jax.experimental import pallas as pl
from jax.experimental.pallas import tpu as pltpu
from jax.sharding import PartitionSpec as P

MESH = pl.DeviceIdType.MESH
BF16, F32 = jnp.bfloat16, jnp.float32

step_size = 8.0
shrink = 0.5

NZ, NY = 16, 4
EXT = 512
NB = 32
HALF = 128
NEAR = 4
FAR = NZ // 2 - NEAR
SIGNS = (1, -1)


def place(rel):
    if abs(rel) == NZ // 2:
        return 0
    far = 2 * (NZ // 2 - abs(rel))
    return far - 1 if rel >= 0 else far


def streams(sign):
    return (0, 1) if sign > 0 else (1, 0)


def far_count(sign, side):
    return FAR if streams(sign)[0] == side else FAR - 1


def dot(a, b, ca=1, cb=0):
    return lax.dot_general(a, b, (((ca,), (cb,)), ((), ())), preferred_element_type=F32)


def kernel(
    pairs,
    live,
    observed,
    common_left,
    common_right,
    innov_left,
    innov_right,
    row_mask,
    col_mask,
    out_common_left,
    out_common_right,
    out_innov_left,
    out_innov_right,
    s,
):
    v = lax.axis_index("vintage")
    t = lax.axis_index("tile")
    z, y = t // NY, t % NY

    def along_z(d):
        return {"tile": lax.rem(z + d + NZ, NZ) * NY + y}

    def along_y(d):
        return {"tile": z * NY + lax.rem(y + d + NY, NY)}

    partner = {"vintage": 1 - v}

    barrier = pltpu.get_barrier_semaphore()
    peers = [along_z(sg * e) for e in range(1, max(FAR, 1) + 1) for sg in SIGNS]
    peers += [along_y(k) for k in range(1, NY)] + [partner]
    for peer in peers:
        pl.semaphore_signal(barrier, inc=1, device_id=peer, device_id_type=MESH)

    load_obs = pltpu.make_async_copy(observed.at[0, 0], s["obs"], s["local_sem"].at[0])
    load_obs.start()

    started = []

    def send(src, dst, dev):
        i = len(started)
        copy = pltpu.make_async_remote_copy(
            src_ref=src,
            dst_ref=dst,
            send_sem=s["send"].at[i],
            recv_sem=s["recv"].at[i],
            device_id=dev,
            device_id_type=MESH,
        )
        copy.start()
        started.append(copy)
        return copy

    def pick(rel, k, slot, side):
        owner = lax.rem(z + rel + NZ, NZ) * NY + lax.rem(y + k, NY)
        return pairs[v, slot, side, owner]

    commons = (common_left, common_right)
    innovs = (innov_left, innov_right)
    for side in range(2):
        for src, dst in ((commons[side], s["common"][side]), (innovs[side], s["innov"][side])):
            x = src[...].astype(F32)
            dst[pl.ds(0, NB * 8, 2), :] = x[:, :HALF]
            dst[pl.ds(1, NB * 8, 2), :] = x[:, HALF:]
        joined = (s["common"][side][...] + s["innov"][side][...]).astype(BF16)
        s["own"][side][...] = joined.reshape(NB, 16, HALF)

    pl.semaphore_wait(barrier, len(peers))

    dense = {}
    for n in range(2):
        for g, sign in enumerate(SIGNS):
            side = streams(sign)[n]
            dense[g, 1, side] = send(s["own"][side], s["dense"][g][0][side], along_z(sign))

    def choose(bufs, o):
        for k in range(NY):
            for side in range(2):
                for slot in range(2):
                    piece = bufs[side][pick(0, k, slot, side)]
                    if k == 0:
                        s["g"][0, o, side, slot] = piece
                    else:
                        s["ysend"][k - 1, o, side, slot] = piece

    arrivals = []

    def spread(o0, n):
        for k in range(1, NY):
            arrivals.append(
                send(s["ysend"].at[k - 1, pl.ds(o0, n)], s["g"].at[k, pl.ds(o0, n)], along_y(k))
            )

    def build_order():
        row = lax.broadcasted_iota(jnp.int32, (EXT, HALF), 0)
        lane = lax.broadcasted_iota(jnp.int32, (EXT, HALF), 1)
        k, o, j = row >> 7, (row >> 3) & 15, row & 7
        dist = NZ // 2 - ((o + 1) >> 1)
        rel = jnp.where((o & 1) == 1, dist, -dist)
        target = 64 * j + ((z + rel + NZ) & (NZ - 1)) * NY + ((y - k + NY) & (NY - 1))
        for c in range(EXT // HALF):
            s["order"][:, c * HALF : (c + 1) * HALF] = jnp.where(
                target == lane + c * HALF, 1.0, 0.0
            ).astype(BF16)

    def order_tile(slot):
        order = s["order"][...]
        turned = dot(order, s["obs"][slot]).astype(BF16)
        for h in range(2):
            cols = slice(h * EXT, (h + 1) * EXT)
            s["obs_o"][slot, :, cols] = dot(turned[:, cols], order, 1, 1).astype(BF16)

    def order_masks(slot):
        order = s["order"][...]
        rows = jnp.broadcast_to(row_mask[slot : slot + 1, :].astype(F32), (HALF, EXT)).astype(BF16)
        cols = jnp.broadcast_to(col_mask[slot : slot + 1, :].astype(F32), (16, EXT)).astype(BF16)
        by_row = dot(order, rows, 1, 1)
        by_col = dot(cols, order, 1, 1)[0:1, :]
        weight = jnp.concatenate([by_row] * (EXT // HALF), axis=1) * by_col
        s["weight"][slot] = (weight * live[v, slot, t].astype(F32)).astype(BF16)

    def one_hot(rel, side):
        row = lax.broadcasted_iota(jnp.int32, (NB * 16, HALF), 0)
        lane = lax.broadcasted_iota(jnp.int32, (1, HALF), 1)
        target = jnp.zeros((1, HALF), jnp.int32)
        for slot in range(2):
            for k in range(NY):
                target = jnp.where(
                    (lane >> 4) == slot * NY + k, pick(rel, k, slot, side), target
                )
        return jnp.where(row == target * 16 + (lane & 15), 1.0, 0.0).astype(BF16)

    def build_own_hot():
        for side in range(2):
            hot = one_hot(0, side)
            s["hot"][side][...] = hot
            for g in range(2):
                s["hot_far"][g][side][:, :HALF] = hot

    def build_far_hot(g):
        sign = SIGNS[g]
        for side in range(2):
            for e in range(1, far_count(sign, side) + 1):
                s["hot_far"][g][side][:, e * HALF : (e + 1) * HALF] = one_hot(-sign * e, side)

    def first_tile():
        load_obs.wait()
        order_tile(0)

    aside = [
        [build_order, first_tile],
        [lambda: order_tile(1)],
        [lambda: order_masks(0), lambda: order_masks(1)],
        [build_own_hot],
        [lambda: build_far_hot(0), lambda: build_far_hot(1)],
    ]
    aside += [[]] * NEAR

    choose(s["own"], place(0))
    spread(place(0), 1)
    for job in aside[0]:
        job()

    picks = {}
    for h in range(1, NEAR + 1):
        for n in range(2):
            for g, sign in enumerate(SIGNS):
                side = streams(sign)[n]
                dense[g, h, side].wait_recv()
                here = s["dense"][g][h - 1][side]
                if h < NEAR:
                    dense[g, h + 1, side] = send(here, s["dense"][g][h][side], along_z(sign))
                else:
                    for e in range(far_count(sign, side), 0, -1):
                        out = s["far_send"][g][side].at[e - 1]
                        for k in range(NY):
                            for slot in range(2):
                                out[k, slot] = here[pick(sign * e, k, slot, side)]
                        picks[g, e, side] = send(out, s["far"][g][side].at[e - 1], along_z(sign * e))
        for g, sign in enumerate(SIGNS):
            choose(s["dense"][g][h - 1], place(-sign * h))
        spread(place(h), 2)
        for job in aside[h]:
            job()
    for jobs in aside[NEAR + 1 : 5]:
        for job in jobs:
            job()

    for e in range(1, FAR + 1):
        d = NEAR + e
        for g, sign in enumerate(SIGNS):
            for side in range(2):
                if e <= far_count(sign, side):
                    picks[g, e, side].wait_recv()
                    o = place(-sign * d)
                    s["g"][0, o, side] = s["far"][g][side][e - 1, 0]
                    for k in range(1, NY):
                        s["ysend"][k - 1, o, side] = s["far"][g][side][e - 1, k]
        spread(place(d), 1 if d == NZ // 2 else 2)
    for copy in arrivals:
        copy.wait_recv()

    def parts(side, slot):
        x = s["g"][:, :, side, slot].reshape(2 * EXT, HALF).astype(F32)
        s["wide"][side][...] = x
        real = s["wide"][side][pl.ds(0, EXT, 2), :].astype(BF16)
        imag = s["wide"][side][pl.ds(1, EXT, 2), :].astype(BF16)
        return real, imag

    def keep(delta, side, slot):
        s["wide"][side][pl.ds(0, EXT, 2), :] = delta[:, :HALF]
        s["wide"][side][pl.ds(1, EXT, 2), :] = delta[:, HALF:]
        pieces = s["wide"][side][...].astype(BF16).reshape(NY, NZ, 16, HALF)
        s["q"][slot, 0, :, side] = pieces[0]
        for k in range(1, NY):
            s["back"][slot, k - 1, :, side] = pieces[k]

    groups = ((0, 3), (3, 4), (7, 4), (11, 5))
    back = {}
    scale = 1.0 / EXT
    for slot in range(2):
        a_re, a_im = parts(0, slot)
        b_re, b_im = parts(1, slot)
        a = jnp.concatenate([a_re, a_im], axis=1)
        s_re = jnp.concatenate([b_re, -b_im], axis=1)
        s_im = jnp.concatenate([b_im, b_re], axis=1)
        t_re = jnp.concatenate([a_re, -a_im], axis=1)
        t_im = jnp.concatenate([a_im, a_re], axis=1)
        weight = s["weight"][slot].astype(F32)
        m_re = (weight * (dot(a, s_re, 1, 1) - s["obs_o"][slot, :, :EXT].astype(F32))).astype(BF16)
        m_im = (weight * (dot(a, s_im, 1, 1) - s["obs_o"][slot, :, EXT:].astype(F32))).astype(BF16)
        keep((dot(m_re, s_re) + dot(m_im, s_im)) * scale, 0, slot)
        keep((dot(m_re, t_re, 0, 0) + dot(m_im, t_im, 0, 0)) * scale, 1, slot)
        for i, (o0, n) in enumerate(groups):
            for k in range(1, NY):
                back[slot, i, k] = send(
                    s["back"].at[slot, k - 1, pl.ds(o0, n)],
                    s["q"].at[slot, k, pl.ds(o0, n)],
                    along_y(-k),
                )

    def arrived(i):
        for slot in range(2):
            for k in range(1, NY):
                back[slot, i, k].wait_recv()

    def own_picks(rel, side):
        return s["q"][:, :, place(rel), side].reshape(HALF, HALF)

    ready = 0
    raw = {}
    for e in range(FAR, 0, -1):
        d = NEAR + e
        while sum(groups[ready - 1]) * (ready > 0) <= place(-d):
            arrived(ready)
            ready += 1
        for n in range(2):
            for g, sign in enumerate(SIGNS):
                side = streams(sign)[n]
                if e <= far_count(sign, side):
                    rows = pl.ds(e * HALF, HALF)
                    s["raw_send"][g][side][rows, :] = own_picks(sign * d, side)
                    raw[g, e, side] = send(
                        s["raw_send"][g][side].at[rows], s["raw"][g][side].at[rows], along_z(sign * e)
                    )
    chain = {}
    while ready < len(groups):
        arrived(ready)
        ready += 1
    for n in range(2):
        for g, sign in enumerate(SIGNS):
            side = streams(sign)[n]
            s["raw"][g][side][0:HALF, :] = own_picks(sign * NEAR, side)
    for n in range(2):
        for g, sign in enumerate(SIGNS):
            side = streams(sign)[n]
            count = far_count(sign, side)
            for e in range(1, count + 1):
                raw[g, e, side].wait_recv()
            depth = (count + 1) * HALF
            total = dot(s["hot_far"][g][side][:, :depth], s["raw"][g][side][0:depth, :])
            s["sum_send"][g][NEAR - 1][side][...] = total.astype(BF16)
            chain[g, NEAR - 1, side] = send(
                s["sum_send"][g][NEAR - 1][side], s["sum"][g][NEAR - 1][side], along_z(sign)
            )
    for h in range(NEAR - 1, 0, -1):
        for side in range(2):
            both = jnp.concatenate([own_picks(h, side), own_picks(-h, side)], axis=1)
            s["add"][side][...] = dot(s["hot"][side][...], both)
        for n in range(2):
            for g, sign in enumerate(SIGNS):
                side = streams(sign)[n]
                chain[g, h, side].wait_recv()
                total = s["sum"][g][h][side][...].astype(F32)
                total = total + s["add"][side][:, g * HALF : (g + 1) * HALF]
                s["sum_send"][g][h - 1][side][...] = total.astype(BF16)
                chain[g, h - 1, side] = send(
                    s["sum_send"][g][h - 1][side], s["sum"][g][h - 1][side], along_z(sign)
                )
    swap = []
    for side in range(2):
        s["grad"][side][...] = dot(s["hot"][side][...], own_picks(0, side))
    for side in range(2):
        for g in range(2):
            chain[g, 0, side].wait_recv()
        s["grad"][side][...] = (
            s["grad"][side][...]
            + s["sum"][0][0][side][...].astype(F32)
            + s["sum"][1][0][side][...].astype(F32)
        )
        swap.append(send(s["grad"][side], s["other"][side], partner))
    for side, out in enumerate((out_innov_left, out_innov_right)):
        innov = s["innov"][side][...]
        out[...] = innov - step_size * (s["grad"][side][...] + shrink * innov)
    for side, out in enumerate((out_common_left, out_common_right)):
        swap[side].wait_recv()
        out[...] = s["common"][side][...] - step_size * (s["grad"][side][...] + s["other"][side][...])
    for copy in started:
        copy.wait_send()


def shard(dtype=BF16):
    return pltpu.VMEM((NB * 16, HALF), dtype)


def scratch():
    blocks = pltpu.VMEM((NB, 16, HALF), BF16)
    exchange = (NZ, 2, 2, 16, HALF)
    copies = 4 * 2 * NEAR + 4 * (4 * FAR - 2) // 2 + (NEAR + FAR + 1) * 3 + 24 + 2
    far = [
        [pltpu.VMEM((far_count(sign, side), NY, 2, 16, HALF), BF16) for side in range(2)]
        for sign in SIGNS
    ]
    raw = [
        [pltpu.VMEM(((far_count(sign, side) + 1) * HALF, HALF), BF16) for side in range(2)]
        for sign in SIGNS
    ]
    hot_far = [
        [pltpu.VMEM((NB * 16, (far_count(sign, side) + 1) * HALF), BF16) for side in range(2)]
        for sign in SIGNS
    ]
    return {
        "common": [shard(F32)] * 2,
        "innov": [shard(F32)] * 2,
        "grad": [shard(F32)] * 2,
        "other": [shard(F32)] * 2,
        "own": [blocks] * 2,
        "dense": [[[blocks] * 2 for _ in range(NEAR)] for _ in range(2)],
        "far_send": far,
        "far": far,
        "ysend": pltpu.VMEM((NY - 1,) + exchange, BF16),
        "g": pltpu.VMEM((NY,) + exchange, BF16),
        "obs": pltpu.VMEM((2, EXT, 2 * EXT), BF16),
        "obs_o": pltpu.VMEM((2, EXT, 2 * EXT), BF16),
        "order": pltpu.VMEM((EXT, EXT), BF16),
        "weight": pltpu.VMEM((2, EXT, EXT), BF16),
        "hot": [shard()] * 2,
        "hot_far": hot_far,
        "wide": [pltpu.VMEM((2 * EXT, HALF), F32)] * 2,
        "back": pltpu.VMEM((2, NY - 1, NZ, 2, 16, HALF), BF16),
        "q": pltpu.VMEM((2, NY, NZ, 2, 16, HALF), BF16),
        "raw_send": raw,
        "raw": raw,
        "sum_send": [[[shard()] * 2 for _ in range(NEAR)] for _ in range(2)],
        "sum": [[[shard()] * 2 for _ in range(NEAR)] for _ in range(2)],
        "add": [pltpu.VMEM((NB * 16, 2 * HALF), F32)] * 2,
        "send": pltpu.SemaphoreType.DMA((copies,)),
        "recv": pltpu.SemaphoreType.DMA((copies,)),
        "local_sem": pltpu.SemaphoreType.DMA((1,)),
    }


def per_device(
    observed,
    common_left,
    common_right,
    innov_left,
    innov_right,
    tile_block_pairs,
    live,
    row_mask,
    col_mask,
):
    rows, width = common_left.shape[0], common_left.shape[2]
    vmem = pl.BlockSpec(memory_space=pltpu.VMEM)
    smem = pl.BlockSpec(memory_space=pltpu.SMEM)
    outs = pl.pallas_call(
        kernel,
        out_shape=[jax.ShapeDtypeStruct((2 * rows, HALF), F32)] * 4,
        in_specs=[smem, smem, pl.BlockSpec(memory_space=pl.ANY)] + [vmem] * 6,
        out_specs=[vmem] * 4,
        scratch_shapes=[scratch()],
        compiler_params=pltpu.CompilerParams(
            collective_id=0, has_side_effects=True, vmem_limit_bytes=56 * 1024 * 1024
        ),
    )(
        tile_block_pairs.transpose(0, 2, 3, 1),
        live.transpose(0, 2, 1),
        observed,
        common_left.reshape(rows, width),
        common_right.reshape(rows, width),
        innov_left.reshape(rows, width),
        innov_right.reshape(rows, width),
        row_mask.reshape(2, EXT),
        col_mask.reshape(2, EXT),
    )
    return (
        outs[0].reshape(rows, 1, width),
        outs[1].reshape(rows, 1, width),
        outs[2].reshape(1, rows, 1, width),
        outs[3].reshape(1, rows, 1, width),
    )


def solution(mesh):
    placed = (
        P("vintage", "tile", "freq", None, None),
        P("freq", "tile", None),
        P("freq", "tile", None),
        P("vintage", "freq", "tile", None),
        P("vintage", "freq", "tile", None),
        P(None, None, "freq", None),
        P(None, None, "freq"),
        P("vintage", "tile", "freq", None),
        P("vintage", "tile", "freq", None),
    )
    return jax.shard_map(
        per_device,
        mesh=mesh,
        in_specs=placed,
        out_specs=(
            P("freq", "tile", None),
            P("freq", "tile", None),
            P("vintage", "freq", "tile", None),
            P("vintage", "freq", "tile", None),
        ),
        check_vma=False,
    )
```

time: 210 us -> 113 us (0.54)
  waiting for transfers between devices: 152 us -> 0 us
  Pallas kernels: 0 us -> 104 us
  starting transfers between devices: 30.6 us -> 0 us
  other arithmetic: 7.9 us -> 0 us
  local copies, waits for them, and re-layouts: 13.2 us -> 7.33 us
  matrix products: 4.61 us -> 0 us
    all_to_all x2 -> x0, waiting for transfers between devices: 152 us -> none  [the longest x1 101 us: per_device(): lax.all_to_all(doubled, ('vintage', 'tile'), split_axis=3, concat_axis=3,...]
    pallas_call x0 -> x1, Pallas kernels: none -> 104 us  [per_device(): pl.pallas_call(kernel, out_shape=[jax.ShapeDtypeStruct((2 * rows, HALF),...]
    all_to_all x2 -> x0, starting transfers between devices: 30.6 us -> none  [the longest x1 19.3 us: per_device(): lax.all_to_all(outgoing, 'tile', split_axis=2, concat_axis=4, tiled=True)]
    dot_general x7 -> x0, matrix products: 4.61 us -> none  [the longest x4 1.93 us: block_sum(): jnp.einsum('bts,sjtc->bjc', onehot, received, preferred_element_type=jnp....]
    concatenate x1 -> x0, other arithmetic: 3.95 us -> none  [per_device(): doubled = jnp.concatenate([going_back, going_back], axis=3)]
    slice x5 -> x0, local copies, waits for them, and re-layouts: 3.62 us -> none  [the longest x1 1.92 us: per_device(): returned_block[:, 1]]
    convert_element_type x5 -> x0, other arithmetic: 2.74 us -> none  [the longest x2 2.01 us: own_blocks(): (common[:, 0].astype(jnp.float32) + innov[0, :, 0].astype(jnp.float32)).a...]
    unnamed x20 -> x4, local copies, waits for them, and re-layouts: 4.82 us -> 7.33 us
  transfers between devices with their start and end apart: 2 -> 0, of which waited for: 2 -> 0; matrix products, arithmetic and copies ran while one was open for 0% -> 0% of each run, Pallas kernels for 0% -> 0%
where the time goes in v1:
time: 113 us; the launch traced here: 112 us
  Pallas kernels  104 us (92%)
  local copies, waits for them, and re-layouts  7.33 us (6%)
    pallas_call x1, Pallas kernels, per_device(): pl.pallas_call(kernel, out_shape=[jax.ShapeDtypeStruct((2 * rows, HALF),...  104 us
    unnamed x4, local copies, waits for them, and re-layouts  7.33 us

profile of v1, /device:TPU:1, one launch (start us, length us, event | category | flops | bytes accessed | tf_op | source)
XLA Modules:
  0.0 112.3 jit_solution(12188026265295823631)
XLA Ops:
  0.6 104.4 %shard_map.120 = (f32[512,128]{1,0:T(8,128)}, f32[512,128]{1,0:T(8,128)}, f32[512,128]{1,0:T(8,128)}, f32[512,128]{1,0:T(8,128)}) custom-call(s32[2,2,2,64]{3,2,1,0:T(2,128)} %bitcast.20, s32[2,2,64]{2,1,0:T(2,128)} %bitcast.23, bf16[1,1,2,512,1024]{4,3,2,1,0:T(8,128)(2,1)} %observed.1, bf16[256,256]{1,0:T(8,128)(2,1)} %bitcast.16, ...), custom_call_target="tpu_custom_call" | custom-call | tf_op jit(solution)/shard_map/pallas_call | solution.py:428
  105.0 1.8 %copy.21 = f32[256,1,256]{2,1,0:T(1,128)} copy(f32[256,1,256]{2,1,0:T(1,128)} %bitcast.15) | data formatting | bytes 524288
  106.8 1.8 %copy.22 = f32[256,1,256]{2,1,0:T(1,128)} copy(f32[256,1,256]{2,1,0:T(1,128)} %bitcast.14) | data formatting | bytes 524288
  108.7 1.8 %copy.23 = f32[1,256,1,256]{3,2,1,0:T(1,128)} copy(f32[1,256,1,256]{3,2,1,0:T(1,128)} %bitcast.13) | data formatting | bytes 524288
  110.5 1.8 %copy.24 = f32[1,256,1,256]{3,2,1,0:T(1,128)} copy(f32[1,256,1,256]{3,2,1,0:T(1,128)} %bitcast.12) | data formatting | bytes 524288

commit v2 on v1

--- a/solution.py
+++ b/solution.py
@@ -15,7 +15,7 @@
 EXT = 512
 NB = 32
 HALF = 128
-NEAR = 4
+NEAR = 3
 FAR = NZ // 2 - NEAR
 SIGNS = (1, -1)
 
@@ -76,7 +76,12 @@
     load_obs = pltpu.make_async_copy(observed.at[0, 0], s["obs"], s["local_sem"].at[0])
     load_obs.start()
 
-    started = []
+    started, gone = [], set()
+
+    def leave(copies):
+        for copy in copies:
+            copy.wait_send()
+            gone.add(id(copy))
 
     def send(src, dst, dev):
         i = len(started)
@@ -109,10 +114,13 @@
     pl.semaphore_wait(barrier, len(peers))
 
     dense = {}
-    for n in range(2):
+
+    def first_hop(n):
         for g, sign in enumerate(SIGNS):
             side = streams(sign)[n]
             dense[g, 1, side] = send(s["own"][side], s["dense"][g][0][side], along_z(sign))
+
+    first_hop(0)
 
     def choose(bufs, o):
         for k in range(NY):
@@ -120,17 +128,21 @@
                 for slot in range(2):
                     piece = bufs[side][pick(0, k, slot, side)]
                     if k == 0:
-                        s["g"][0, o, side, slot] = piece
+                        s["g"][slot, 0, o, side] = piece
                     else:
-                        s["ysend"][k - 1, o, side, slot] = piece
-
-    arrivals = []
-
-    def spread(o0, n):
-        for k in range(1, NY):
-            arrivals.append(
-                send(s["ysend"].at[k - 1, pl.ds(o0, n)], s["g"].at[k, pl.ds(o0, n)], along_y(k))
+                        s["ysend"][slot, k - 1, o, side] = piece
+
+    def spread(slots, o0, n):
+        return [
+            send(
+                s["ysend"].at[slots, k - 1, pl.ds(o0, n)],
+                s["g"].at[slots, k, pl.ds(o0, n)],
+                along_y(k),
             )
+            for k in range(1, NY)
+        ]
+
+    both_slots = pl.ds(0, 2)
 
     def build_order():
         row = lax.broadcasted_iota(jnp.int32, (EXT, HALF), 0)
@@ -189,60 +201,74 @@
         order_tile(0)
 
     aside = [
-        [build_order, first_tile],
         [lambda: order_tile(1)],
         [lambda: order_masks(0), lambda: order_masks(1)],
-        [build_own_hot],
-        [lambda: build_far_hot(0), lambda: build_far_hot(1)],
+        [build_own_hot, lambda: build_far_hot(0)],
+        [lambda: build_far_hot(1)],
     ]
-    aside += [[]] * NEAR
 
     choose(s["own"], place(0))
-    spread(place(0), 1)
-    for job in aside[0]:
-        job()
+    near = spread(both_slots, place(0), 1)
+    build_order()
+    leave([dense[g, 1, streams(sign)[0]] for g, sign in enumerate(SIGNS)])
+    first_hop(1)
+    first_tile()
 
     picks = {}
+
+    def pick_far(g, side, slot):
+        sign = SIGNS[g]
+        here = s["dense"][g][NEAR - 1][side]
+        for e in range(far_count(sign, side), 0, -1):
+            out = s["far_send"][g][side].at[slot, e - 1]
+            for k in range(NY):
+                out[k] = here[pick(sign * e, k, slot, side)]
+            picks[g, e, side, slot] = send(
+                out, s["far"][g][side].at[slot, e - 1], along_z(sign * e)
+            )
+
     for h in range(1, NEAR + 1):
         for n in range(2):
             for g, sign in enumerate(SIGNS):
                 side = streams(sign)[n]
                 dense[g, h, side].wait_recv()
-                here = s["dense"][g][h - 1][side]
                 if h < NEAR:
-                    dense[g, h + 1, side] = send(here, s["dense"][g][h][side], along_z(sign))
+                    dense[g, h + 1, side] = send(
+                        s["dense"][g][h - 1][side], s["dense"][g][h][side], along_z(sign)
+                    )
                 else:
-                    for e in range(far_count(sign, side), 0, -1):
-                        out = s["far_send"][g][side].at[e - 1]
-                        for k in range(NY):
-                            for slot in range(2):
-                                out[k, slot] = here[pick(sign * e, k, slot, side)]
-                        picks[g, e, side] = send(out, s["far"][g][side].at[e - 1], along_z(sign * e))
+                    pick_far(g, side, 0)
+            if n == 0 and h < NEAR and aside:
+                for job in aside.pop(0):
+                    job()
         for g, sign in enumerate(SIGNS):
             choose(s["dense"][g][h - 1], place(-sign * h))
-        spread(place(h), 2)
-        for job in aside[h]:
-            job()
-    for jobs in aside[NEAR + 1 : 5]:
+        near += spread(both_slots, place(h), 2)
+    for jobs in aside:
         for job in jobs:
             job()
-
-    for e in range(1, FAR + 1):
-        d = NEAR + e
+    leave([picks[key] for key in picks if key[3] == 0])
+    for n in range(2):
         for g, sign in enumerate(SIGNS):
-            for side in range(2):
-                if e <= far_count(sign, side):
-                    picks[g, e, side].wait_recv()
-                    o = place(-sign * d)
-                    s["g"][0, o, side] = s["far"][g][side][e - 1, 0]
-                    for k in range(1, NY):
-                        s["ysend"][k - 1, o, side] = s["far"][g][side][e - 1, k]
-        spread(place(d), 1 if d == NZ // 2 else 2)
-    for copy in arrivals:
-        copy.wait_recv()
+            pick_far(g, streams(sign)[n], 1)
+
+    def far_in(slot):
+        copies = []
+        for e in range(FAR, 0, -1):
+            d = NEAR + e
+            for g, sign in enumerate(SIGNS):
+                for side in range(2):
+                    if e <= far_count(sign, side):
+                        picks[g, e, side, slot].wait_recv()
+                        o = place(-sign * d)
+                        s["g"][slot, 0, o, side] = s["far"][g][side][slot, e - 1, 0]
+                        for k in range(1, NY):
+                            s["ysend"][slot, k - 1, o, side] = s["far"][g][side][slot, e - 1, k]
+            copies += spread(slot, place(d), 1 if d == NZ // 2 else 2)
+        return copies
 
     def parts(side, slot):
-        x = s["g"][:, :, side, slot].reshape(2 * EXT, HALF).astype(F32)
+        x = s["g"][slot, :, :, side].reshape(2 * EXT, HALF).astype(F32)
         s["wide"][side][...] = x
         real = s["wide"][side][pl.ds(0, EXT, 2), :].astype(BF16)
         imag = s["wide"][side][pl.ds(1, EXT, 2), :].astype(BF16)
@@ -256,10 +282,11 @@
         for k in range(1, NY):
             s["back"][slot, k - 1, :, side] = pieces[k]
 
-    groups = ((0, 3), (3, 4), (7, 4), (11, 5))
+    groups = ((0, 3), (3, 2 * FAR - 4), (2 * FAR - 1, 4), (2 * FAR + 3, 2 * NEAR - 3))
     back = {}
     scale = 1.0 / EXT
-    for slot in range(2):
+
+    def tile(slot):
         a_re, a_im = parts(0, slot)
         b_re, b_im = parts(1, slot)
         a = jnp.concatenate([a_re, a_im], axis=1)
@@ -280,67 +307,85 @@
                     along_y(-k),
                 )
 
-    def arrived(i):
-        for slot in range(2):
-            for k in range(1, NY):
-                back[slot, i, k].wait_recv()
+    def arrived(slot, i):
+        for k in range(1, NY):
+            back[slot, i, k].wait_recv()
 
     def own_picks(rel, side):
         return s["q"][:, :, place(rel), side].reshape(HALF, HALF)
 
-    ready = 0
     raw = {}
-    for e in range(FAR, 0, -1):
-        d = NEAR + e
-        while sum(groups[ready - 1]) * (ready > 0) <= place(-d):
-            arrived(ready)
-            ready += 1
+
+    def far_out(slot):
+        arrived(slot, 0)
+        arrived(slot, 1)
         for n in range(2):
             for g, sign in enumerate(SIGNS):
                 side = streams(sign)[n]
-                if e <= far_count(sign, side):
-                    rows = pl.ds(e * HALF, HALF)
-                    s["raw_send"][g][side][rows, :] = own_picks(sign * d, side)
-                    raw[g, e, side] = send(
+                for e in range(far_count(sign, side), 0, -1):
+                    rows = pl.ds(e * HALF + slot * (HALF // 2), HALF // 2)
+                    mine = s["q"][slot, :, place(sign * (NEAR + e)), side]
+                    s["raw_send"][g][side][rows, :] = mine.reshape(HALF // 2, HALF)
+                    raw[g, e, side, slot] = send(
                         s["raw_send"][g][side].at[rows], s["raw"][g][side].at[rows], along_z(sign * e)
                     )
+
+    early = far_in(0)
+    for copy in near + early:
+        copy.wait_recv()
+    tile(0)
+    late = far_in(1)
+    far_out(0)
+    for copy in late:
+        copy.wait_recv()
+    tile(1)
+    far_out(1)
+    for slot in range(2):
+        arrived(slot, 2)
+    for g, sign in enumerate(SIGNS):
+        for side in range(2):
+            s["raw"][g][side][0:HALF, :] = own_picks(sign * NEAR, side)
+
+    def own_sums(h):
+        for side in range(2):
+            both = jnp.concatenate([own_picks(h, side), own_picks(-h, side)], axis=1)
+            s["add"][h - 1][side][...] = dot(s["hot"][side][...], both)
+
+    own_sums(NEAR - 1)
     chain = {}
-    while ready < len(groups):
-        arrived(ready)
-        ready += 1
-    for n in range(2):
-        for g, sign in enumerate(SIGNS):
-            side = streams(sign)[n]
-            s["raw"][g][side][0:HALF, :] = own_picks(sign * NEAR, side)
     for n in range(2):
         for g, sign in enumerate(SIGNS):
             side = streams(sign)[n]
             count = far_count(sign, side)
-            for e in range(1, count + 1):
-                raw[g, e, side].wait_recv()
+            for e in range(count, 0, -1):
+                for slot in range(2):
+                    raw[g, e, side, slot].wait_recv()
             depth = (count + 1) * HALF
             total = dot(s["hot_far"][g][side][:, :depth], s["raw"][g][side][0:depth, :])
             s["sum_send"][g][NEAR - 1][side][...] = total.astype(BF16)
+            if n == 1:
+                leave([chain[g, NEAR - 1, streams(sign)[0]]])
             chain[g, NEAR - 1, side] = send(
                 s["sum_send"][g][NEAR - 1][side], s["sum"][g][NEAR - 1][side], along_z(sign)
             )
+    for slot in range(2):
+        arrived(slot, 3)
+    for h in range(NEAR - 2, 0, -1):
+        own_sums(h)
+    for side in range(2):
+        s["grad"][side][...] = dot(s["hot"][side][...], own_picks(0, side))
     for h in range(NEAR - 1, 0, -1):
-        for side in range(2):
-            both = jnp.concatenate([own_picks(h, side), own_picks(-h, side)], axis=1)
-            s["add"][side][...] = dot(s["hot"][side][...], both)
         for n in range(2):
             for g, sign in enumerate(SIGNS):
                 side = streams(sign)[n]
                 chain[g, h, side].wait_recv()
                 total = s["sum"][g][h][side][...].astype(F32)
-                total = total + s["add"][side][:, g * HALF : (g + 1) * HALF]
+                total = total + s["add"][h - 1][side][:, g * HALF : (g + 1) * HALF]
                 s["sum_send"][g][h - 1][side][...] = total.astype(BF16)
                 chain[g, h - 1, side] = send(
                     s["sum_send"][g][h - 1][side], s["sum"][g][h - 1][side], along_z(sign)
                 )
     swap = []
-    for side in range(2):
-        s["grad"][side][...] = dot(s["hot"][side][...], own_picks(0, side))
     for side in range(2):
         for g in range(2):
             chain[g, 0, side].wait_recv()
@@ -356,8 +401,20 @@
     for side, out in enumerate((out_common_left, out_common_right)):
         swap[side].wait_recv()
         out[...] = s["common"][side][...] - step_size * (s["grad"][side][...] + s["other"][side][...])
-    for copy in started:
-        copy.wait_send()
+    leave([copy for copy in started if id(copy) not in gone])
+
+
+def hand_over(*refs):
+    given, outs, held, sems = refs[:4], refs[4:8], refs[8], refs[9]
+    inward = [pltpu.make_async_copy(given[i], held.at[i], sems.at[i]) for i in range(4)]
+    outward = [pltpu.make_async_copy(held.at[i], outs[i], sems.at[4 + i]) for i in range(4)]
+    for copy in inward:
+        copy.start()
+    for i in range(4):
+        inward[i].wait()
+        outward[i].start()
+    for copy in outward:
+        copy.wait()
 
 
 def shard(dtype=BF16):
@@ -366,10 +423,10 @@
 
 def scratch():
     blocks = pltpu.VMEM((NB, 16, HALF), BF16)
-    exchange = (NZ, 2, 2, 16, HALF)
-    copies = 4 * 2 * NEAR + 4 * (4 * FAR - 2) // 2 + (NEAR + FAR + 1) * 3 + 24 + 2
+    exchange = (NZ, 2, 16, HALF)
+    copies = 8 * NEAR + 4 * (4 * FAR - 2) + (NEAR + 2 * FAR + 1) * 3 + 24 + 2
     far = [
-        [pltpu.VMEM((far_count(sign, side), NY, 2, 16, HALF), BF16) for side in range(2)]
+        [pltpu.VMEM((2, far_count(sign, side), NY, 16, HALF), BF16) for side in range(2)]
         for sign in SIGNS
     ]
     raw = [
@@ -389,8 +446,8 @@
         "dense": [[[blocks] * 2 for _ in range(NEAR)] for _ in range(2)],
         "far_send": far,
         "far": far,
-        "ysend": pltpu.VMEM((NY - 1,) + exchange, BF16),
-        "g": pltpu.VMEM((NY,) + exchange, BF16),
+        "ysend": pltpu.VMEM((2, NY - 1) + exchange, BF16),
+        "g": pltpu.VMEM((2, NY) + exchange, BF16),
         "obs": pltpu.VMEM((2, EXT, 2 * EXT), BF16),
         "obs_o": pltpu.VMEM((2, EXT, 2 * EXT), BF16),
         "order": pltpu.VMEM((EXT, EXT), BF16),
@@ -398,13 +455,13 @@
         "hot": [shard()] * 2,
         "hot_far": hot_far,
         "wide": [pltpu.VMEM((2 * EXT, HALF), F32)] * 2,
-        "back": pltpu.VMEM((2, NY - 1, NZ, 2, 16, HALF), BF16),
-        "q": pltpu.VMEM((2, NY, NZ, 2, 16, HALF), BF16),
+        "back": pltpu.VMEM((2, NY - 1) + exchange, BF16),
+        "q": pltpu.VMEM((2, NY) + exchange, BF16),
         "raw_send": raw,
         "raw": raw,
         "sum_send": [[[shard()] * 2 for _ in range(NEAR)] for _ in range(2)],
         "sum": [[[shard()] * 2 for _ in range(NEAR)] for _ in range(2)],
-        "add": [pltpu.VMEM((NB * 16, 2 * HALF), F32)] * 2,
+        "add": [[pltpu.VMEM((NB * 16, 2 * HALF), F32)] * 2 for _ in range(NEAR - 1)],
         "send": pltpu.SemaphoreType.DMA((copies,)),
         "recv": pltpu.SemaphoreType.DMA((copies,)),
         "local_sem": pltpu.SemaphoreType.DMA((1,)),
@@ -445,6 +502,14 @@
         row_mask.reshape(2, EXT),
         col_mask.reshape(2, EXT),
     )
+    outs = pl.pallas_call(
+        hand_over,
+        out_shape=[jax.ShapeDtypeStruct((2 * rows, HALF), F32)] * 4,
+        in_specs=[pl.BlockSpec(memory_space=pl.ANY)] * 4,
+        out_specs=[pl.BlockSpec(memory_space=pl.ANY)] * 4,
+        scratch_shapes=[pltpu.VMEM((4, 2 * rows, HALF), F32), pltpu.SemaphoreType.DMA((8,))],
+        compiler_params=pltpu.CompilerParams(vmem_limit_bytes=56 * 1024 * 1024),
+    )(*outs)
     return (
         outs[0].reshape(rows, 1, width),
         outs[1].reshape(rows, 1, width),

time: 113 us -> 104 us (0.920)
  local copies, waits for them, and re-layouts: 7.33 us -> 0 us
    unnamed x4 -> x0, local copies, waits for them, and re-layouts: 7.33 us -> none
    pallas_call x1, Pallas kernels: 104 us -> 101 us  [per_device(): pl.pallas_call(kernel, out_shape=[jax.ShapeDtypeStruct((2 * rows, HALF),...]
    pallas_call x0 -> x1, Pallas kernels: none -> 1.98 us  [per_device(): pl.pallas_call(hand_over, out_shape=[jax.ShapeDtypeStruct((2 * rows, HALF...]
where the time goes in v2:
time: 104 us
  Pallas kernels  103 us (99%)
    pallas_call x1, Pallas kernels, per_device(): pl.pallas_call(kernel, out_shape=[jax.ShapeDtypeStruct((2 * rows, HALF),...  101 us

profile of v2, /device:TPU:1, one launch (start us, length us, event | category | flops | bytes accessed | tf_op | source)
XLA Modules:
  0.0 104.1 jit_solution(9409290657196514211)
XLA Ops:
  0.6 101.5 %shard_map.120 = (f32[512,128]{1,0:T(8,128)}, f32[512,128]{1,0:T(8,128)}, f32[512,128]{1,0:T(8,128)}, f32[512,128]{1,0:T(8,128)}) custom-call(s32[2,2,2,64]{3,2,1,0:T(2,128)} %bitcast.16, s32[2,2,64]{2,1,0:T(2,128)} %bitcast.19, bf16[1,1,2,512,1024]{4,3,2,1,0:T(8,128)(2,1)} %observed.1, bf16[256,256]{1,0:T(8,128)(2,1)} %bitcast.12, ...), custom_call_target="tpu_custom_call" | custom-call | tf_op jit(solution)/shard_map/pallas_call | solution.py:485
  102.1 2.0 %shard_map.121 = (f32[512,128]{1,0:T(8,128)}, f32[512,128]{1,0:T(8,128)}, f32[512,128]{1,0:T(8,128)}, f32[512,128]{1,0:T(8,128)}) custom-call(f32[512,128]{1,0:T(8,128)} %get-tuple-element.12.refs_0_, f32[512,128]{1,0:T(8,128)} %get-tuple-element.13.refs_1_, f32[512,128]{1,0:T(8,128)} %get-tuple-element.14.refs_2_, f32[512,128]{1,0:T(8,128)} %get-tuple-element.15.refs_3_), custom_call_target="tpu_custom_call" | custom-call | tf_op jit(solution)/shard_map/pallas_call | solution.py:505

commit v3 on v2

--- a/solution.py
+++ b/solution.py
@@ -18,6 +18,8 @@
 NEAR = 3
 FAR = NZ // 2 - NEAR
 SIGNS = (1, -1)
+HALVES = (pl.ds(0, NB // 2), pl.ds(NB // 2, NB // 2))
+ROWS = (pl.ds(0, NB * 8), pl.ds(NB * 8, NB * 8))
 
 
 def place(rel):
@@ -118,7 +120,10 @@
     def first_hop(n):
         for g, sign in enumerate(SIGNS):
             side = streams(sign)[n]
-            dense[g, 1, side] = send(s["own"][side], s["dense"][g][0][side], along_z(sign))
+            for c, blocks in enumerate(HALVES):
+                dense[g, 1, side, c] = send(
+                    s["own"][side].at[blocks], s["dense"][g][0][side].at[blocks], along_z(sign)
+                )
 
     first_hop(0)
 
@@ -196,23 +201,11 @@
             for e in range(1, far_count(sign, side) + 1):
                 s["hot_far"][g][side][:, e * HALF : (e + 1) * HALF] = one_hot(-sign * e, side)
 
-    def first_tile():
-        load_obs.wait()
-        order_tile(0)
-
-    aside = [
-        [lambda: order_tile(1)],
-        [lambda: order_masks(0), lambda: order_masks(1)],
-        [build_own_hot, lambda: build_far_hot(0)],
-        [lambda: build_far_hot(1)],
-    ]
-
     choose(s["own"], place(0))
     near = spread(both_slots, place(0), 1)
     build_order()
-    leave([dense[g, 1, streams(sign)[0]] for g, sign in enumerate(SIGNS)])
+    leave([dense[g, 1, streams(sign)[0], c] for c in range(2) for g, sign in enumerate(SIGNS)])
     first_hop(1)
-    first_tile()
 
     picks = {}
 
@@ -229,28 +222,31 @@
 
     for h in range(1, NEAR + 1):
         for n in range(2):
-            for g, sign in enumerate(SIGNS):
-                side = streams(sign)[n]
-                dense[g, h, side].wait_recv()
-                if h < NEAR:
-                    dense[g, h + 1, side] = send(
-                        s["dense"][g][h - 1][side], s["dense"][g][h][side], along_z(sign)
-                    )
-                else:
-                    pick_far(g, side, 0)
-            if n == 0 and h < NEAR and aside:
-                for job in aside.pop(0):
-                    job()
+            for c, blocks in enumerate(HALVES):
+                for g, sign in enumerate(SIGNS):
+                    side = streams(sign)[n]
+                    dense[g, h, side, c].wait_recv()
+                    if h < NEAR:
+                        dense[g, h + 1, side, c] = send(
+                            s["dense"][g][h - 1][side].at[blocks],
+                            s["dense"][g][h][side].at[blocks],
+                            along_z(sign),
+                        )
+            if h == NEAR:
+                for g, sign in enumerate(SIGNS):
+                    pick_far(g, streams(sign)[n], 0)
         for g, sign in enumerate(SIGNS):
             choose(s["dense"][g][h - 1], place(-sign * h))
         near += spread(both_slots, place(h), 2)
-    for jobs in aside:
-        for job in jobs:
-            job()
+    load_obs.wait()
+    order_tile(0)
+    order_masks(0)
     leave([picks[key] for key in picks if key[3] == 0])
     for n in range(2):
         for g, sign in enumerate(SIGNS):
             pick_far(g, streams(sign)[n], 1)
+    order_tile(1)
+    order_masks(1)
 
     def far_in(slot):
         copies = []
@@ -334,12 +330,15 @@
     for copy in near + early:
         copy.wait_recv()
     tile(0)
+    build_own_hot()
     late = far_in(1)
     far_out(0)
     for copy in late:
         copy.wait_recv()
     tile(1)
     far_out(1)
+    for g in range(2):
+        build_far_hot(g)
     for slot in range(2):
         arrived(slot, 2)
     for g, sign in enumerate(SIGNS):
@@ -353,6 +352,12 @@
 
     own_sums(NEAR - 1)
     chain = {}
+
+    def pass_on(g, h, side, c):
+        chain[g, h, side, c] = send(
+            s["sum_send"][g][h][side].at[ROWS[c]], s["sum"][g][h][side].at[ROWS[c]], along_z(SIGNS[g])
+        )
+
     for n in range(2):
         for g, sign in enumerate(SIGNS):
             side = streams(sign)[n]
@@ -360,14 +365,15 @@
             for e in range(count, 0, -1):
                 for slot in range(2):
                     raw[g, e, side, slot].wait_recv()
-            depth = (count + 1) * HALF
-            total = dot(s["hot_far"][g][side][:, :depth], s["raw"][g][side][0:depth, :])
-            s["sum_send"][g][NEAR - 1][side][...] = total.astype(BF16)
-            if n == 1:
-                leave([chain[g, NEAR - 1, streams(sign)[0]]])
-            chain[g, NEAR - 1, side] = send(
-                s["sum_send"][g][NEAR - 1][side], s["sum"][g][NEAR - 1][side], along_z(sign)
-            )
+        for c, rows in enumerate(ROWS):
+            for g, sign in enumerate(SIGNS):
+                side = streams(sign)[n]
+                depth = (far_count(sign, side) + 1) * HALF
+                total = dot(s["hot_far"][g][side][rows, :depth], s["raw"][g][side][0:depth, :])
+                s["sum_send"][g][NEAR - 1][side][rows, :] = total.astype(BF16)
+                if n == 1:
+                    leave([chain[g, NEAR - 1, streams(sign)[0], c]])
+                pass_on(g, NEAR - 1, side, c)
     for slot in range(2):
         arrived(slot, 3)
     for h in range(NEAR - 2, 0, -1):
@@ -376,31 +382,34 @@
         s["grad"][side][...] = dot(s["hot"][side][...], own_picks(0, side))
     for h in range(NEAR - 1, 0, -1):
         for n in range(2):
-            for g, sign in enumerate(SIGNS):
-                side = streams(sign)[n]
-                chain[g, h, side].wait_recv()
-                total = s["sum"][g][h][side][...].astype(F32)
-                total = total + s["add"][h - 1][side][:, g * HALF : (g + 1) * HALF]
-                s["sum_send"][g][h - 1][side][...] = total.astype(BF16)
-                chain[g, h - 1, side] = send(
-                    s["sum_send"][g][h - 1][side], s["sum"][g][h - 1][side], along_z(sign)
-                )
-    swap = []
-    for side in range(2):
-        for g in range(2):
-            chain[g, 0, side].wait_recv()
-        s["grad"][side][...] = (
-            s["grad"][side][...]
-            + s["sum"][0][0][side][...].astype(F32)
-            + s["sum"][1][0][side][...].astype(F32)
-        )
-        swap.append(send(s["grad"][side], s["other"][side], partner))
+            for c, rows in enumerate(ROWS):
+                for g, sign in enumerate(SIGNS):
+                    side = streams(sign)[n]
+                    chain[g, h, side, c].wait_recv()
+                    total = s["sum"][g][h][side][rows, :].astype(F32)
+                    total = total + s["add"][h - 1][side][rows, g * HALF : (g + 1) * HALF]
+                    s["sum_send"][g][h - 1][side][rows, :] = total.astype(BF16)
+                    pass_on(g, h - 1, side, c)
+    swap = {}
+    for c, rows in enumerate(ROWS):
+        for side in range(2):
+            for g in range(2):
+                chain[g, 0, side, c].wait_recv()
+            s["grad"][side][rows, :] = (
+                s["grad"][side][rows, :]
+                + s["sum"][0][0][side][rows, :].astype(F32)
+                + s["sum"][1][0][side][rows, :].astype(F32)
+            )
+            swap[side, c] = send(s["grad"][side].at[rows], s["other"][side].at[rows], partner)
     for side, out in enumerate((out_innov_left, out_innov_right)):
         innov = s["innov"][side][...]
         out[...] = innov - step_size * (s["grad"][side][...] + shrink * innov)
-    for side, out in enumerate((out_common_left, out_common_right)):
-        swap[side].wait_recv()
-        out[...] = s["common"][side][...] - step_size * (s["grad"][side][...] + s["other"][side][...])
+    for c, rows in enumerate(ROWS):
+        for side, out in enumerate((out_common_left, out_common_right)):
+            swap[side, c].wait_recv()
+            out[rows, :] = s["common"][side][rows, :] - step_size * (
+                s["grad"][side][rows, :] + s["other"][side][rows, :]
+            )
     leave([copy for copy in started if id(copy) not in gone])
 
 
@@ -424,7 +433,7 @@
 def scratch():
     blocks = pltpu.VMEM((NB, 16, HALF), BF16)
     exchange = (NZ, 2, 16, HALF)
-    copies = 8 * NEAR + 4 * (4 * FAR - 2) + (NEAR + 2 * FAR + 1) * 3 + 24 + 2
+    copies = 16 * NEAR + 4 * (4 * FAR - 2) + (NEAR + 2 * FAR + 1) * 3 + 24 + 4
     far = [
         [pltpu.VMEM((2, far_count(sign, side), NY, 16, HALF), BF16) for side in range(2)]
         for sign in SIGNS

time: 104 us -> 103 us (level)
    pallas_call x1, Pallas kernels: 101 us -> 100 us  [per_device(): pl.pallas_call(kernel, out_shape=[jax.ShapeDtypeStruct((2 * rows, HALF),...]
where the time goes in v3:
time: 103 us
  Pallas kernels  102 us (99%)
    pallas_call x1, Pallas kernels, per_device(): pl.pallas_call(kernel, out_shape=[jax.ShapeDtypeStruct((2 * rows, HALF),...  100 us

profile of v3, /device:TPU:1, one launch (start us, length us, event | category | flops | bytes accessed | tf_op | source)
XLA Modules:
  0.0 103.1 jit_solution(17209309825988107567)
XLA Ops:
  0.6 100.5 %shard_map.120 = (f32[512,128]{1,0:T(8,128)}, f32[512,128]{1,0:T(8,128)}, f32[512,128]{1,0:T(8,128)}, f32[512,128]{1,0:T(8,128)}) custom-call(s32[2,2,2,64]{3,2,1,0:T(2,128)} %bitcast.16, s32[2,2,64]{2,1,0:T(2,128)} %bitcast.19, bf16[1,1,2,512,1024]{4,3,2,1,0:T(8,128)(2,1)} %observed.1, bf16[256,256]{1,0:T(8,128)(2,1)} %bitcast.12, ...), custom_call_target="tpu_custom_call" | custom-call | tf_op jit(solution)/shard_map/pallas_call | solution.py:494
  101.1 2.0 %shard_map.121 = (f32[512,128]{1,0:T(8,128)}, f32[512,128]{1,0:T(8,128)}, f32[512,128]{1,0:T(8,128)}, f32[512,128]{1,0:T(8,128)}) custom-call(f32[512,128]{1,0:T(8,128)} %get-tuple-element.12.refs_0_, f32[512,128]{1,0:T(8,128)} %get-tuple-element.13.refs_1_, f32[512,128]{1,0:T(8,128)} %get-tuple-element.14.refs_2_, f32[512,128]{1,0:T(8,128)} %get-tuple-element.15.refs_3_), custom_call_target="tpu_custom_call" | custom-call | tf_op jit(solution)/shard_map/pallas_call | solution.py:514

commit v4 on v3

--- a/solution.py
+++ b/solution.py
@@ -29,12 +29,8 @@
     return far - 1 if rel >= 0 else far
 
 
-def streams(sign):
-    return (0, 1) if sign > 0 else (1, 0)
-
-
 def far_count(sign, side):
-    return FAR if streams(sign)[0] == side else FAR - 1
+    return FAR if (sign > 0) == (side == 0) else FAR - 1
 
 
 def dot(a, b, ca=1, cb=0):
@@ -117,10 +113,9 @@
 
     dense = {}
 
-    def first_hop(n):
-        for g, sign in enumerate(SIGNS):
-            side = streams(sign)[n]
-            for c, blocks in enumerate(HALVES):
+    def first_hop(side):
+        for c, blocks in enumerate(HALVES):
+            for g, sign in enumerate(SIGNS):
                 dense[g, 1, side, c] = send(
                     s["own"][side].at[blocks], s["dense"][g][0][side].at[blocks], along_z(sign)
                 )
@@ -204,27 +199,31 @@
     choose(s["own"], place(0))
     near = spread(both_slots, place(0), 1)
     build_order()
-    leave([dense[g, 1, streams(sign)[0], c] for c in range(2) for g, sign in enumerate(SIGNS)])
+    leave([dense[g, 1, 0, c] for c in range(2) for g in range(2)])
     first_hop(1)
 
     picks = {}
 
-    def pick_far(g, side, slot):
-        sign = SIGNS[g]
+    def stage_far(g, side, slot):
         here = s["dense"][g][NEAR - 1][side]
-        for e in range(far_count(sign, side), 0, -1):
-            out = s["far_send"][g][side].at[slot, e - 1]
+        for e in range(far_count(SIGNS[g], side), 0, -1):
             for k in range(NY):
-                out[k] = here[pick(sign * e, k, slot, side)]
-            picks[g, e, side, slot] = send(
-                out, s["far"][g][side].at[slot, e - 1], along_z(sign * e)
-            )
+                s["far_send"][g][side][slot, e - 1, k] = here[pick(SIGNS[g] * e, k, slot, side)]
+
+    def send_far(side, slot):
+        for e in range(FAR, 0, -1):
+            for g, sign in enumerate(SIGNS):
+                if e <= far_count(sign, side):
+                    picks[g, e, side, slot] = send(
+                        s["far_send"][g][side].at[slot, e - 1],
+                        s["far"][g][side].at[slot, e - 1],
+                        along_z(sign * e),
+                    )
 
     for h in range(1, NEAR + 1):
-        for n in range(2):
+        for side in range(2):
             for c, blocks in enumerate(HALVES):
                 for g, sign in enumerate(SIGNS):
-                    side = streams(sign)[n]
                     dense[g, h, side, c].wait_recv()
                     if h < NEAR:
                         dense[g, h + 1, side, c] = send(
@@ -233,18 +232,21 @@
                             along_z(sign),
                         )
             if h == NEAR:
-                for g, sign in enumerate(SIGNS):
-                    pick_far(g, streams(sign)[n], 0)
+                for g in range(2):
+                    stage_far(g, side, 0)
+                send_far(side, 0)
         for g, sign in enumerate(SIGNS):
             choose(s["dense"][g][h - 1], place(-sign * h))
         near += spread(both_slots, place(h), 2)
+    for side in range(2):
+        for g in range(2):
+            stage_far(g, side, 1)
     load_obs.wait()
     order_tile(0)
+    leave([picks[key] for key in picks if key[3] == 0])
+    for side in range(2):
+        send_far(side, 1)
     order_masks(0)
-    leave([picks[key] for key in picks if key[3] == 0])
-    for n in range(2):
-        for g, sign in enumerate(SIGNS):
-            pick_far(g, streams(sign)[n], 1)
     order_tile(1)
     order_masks(1)
 
@@ -274,12 +276,20 @@
         s["wide"][side][pl.ds(0, EXT, 2), :] = delta[:, :HALF]
         s["wide"][side][pl.ds(1, EXT, 2), :] = delta[:, HALF:]
         pieces = s["wide"][side][...].astype(BF16).reshape(NY, NZ, 16, HALF)
-        s["q"][slot, 0, :, side] = pieces[0]
+        s["q"][slot, 0, side] = pieces[0]
         for k in range(1, NY):
-            s["back"][slot, k - 1, :, side] = pieces[k]
-
-    groups = ((0, 3), (3, 2 * FAR - 4), (2 * FAR - 1, 4), (2 * FAR + 3, 2 * NEAR - 3))
+            s["back"][slot, k - 1, side] = pieces[k]
+
     back = {}
+
+    def give_back(slot, i, sides, o0, n):
+        for k in (2, 1, 3):
+            back[slot, i, k] = send(
+                s["back"].at[slot, k - 1, sides, pl.ds(o0, n)],
+                s["q"].at[slot, k, sides, pl.ds(o0, n)],
+                along_y(-k),
+            )
+
     scale = 1.0 / EXT
 
     def tile(slot):
@@ -294,37 +304,35 @@
         m_re = (weight * (dot(a, s_re, 1, 1) - s["obs_o"][slot, :, :EXT].astype(F32))).astype(BF16)
         m_im = (weight * (dot(a, s_im, 1, 1) - s["obs_o"][slot, :, EXT:].astype(F32))).astype(BF16)
         keep((dot(m_re, s_re) + dot(m_im, s_im)) * scale, 0, slot)
+        give_back(slot, 0, 0, 0, 2 * FAR - 1)
         keep((dot(m_re, t_re, 0, 0) + dot(m_im, t_im, 0, 0)) * scale, 1, slot)
-        for i, (o0, n) in enumerate(groups):
-            for k in range(1, NY):
-                back[slot, i, k] = send(
-                    s["back"].at[slot, k - 1, pl.ds(o0, n)],
-                    s["q"].at[slot, k, pl.ds(o0, n)],
-                    along_y(-k),
-                )
+        give_back(slot, 1, 1, 0, 2 * FAR - 1)
+        give_back(slot, 2, pl.ds(0, 2), 2 * FAR - 1, 4)
+        give_back(slot, 3, pl.ds(0, 2), 2 * FAR + 3, 2 * NEAR - 3)
 
     def arrived(slot, i):
         for k in range(1, NY):
             back[slot, i, k].wait_recv()
 
     def own_picks(rel, side):
-        return s["q"][:, :, place(rel), side].reshape(HALF, HALF)
+        return s["q"][:, :, side, place(rel)].reshape(HALF, HALF)
 
     raw = {}
 
     def far_out(slot):
-        arrived(slot, 0)
-        arrived(slot, 1)
-        for n in range(2):
-            for g, sign in enumerate(SIGNS):
-                side = streams(sign)[n]
-                for e in range(far_count(sign, side), 0, -1):
-                    rows = pl.ds(e * HALF + slot * (HALF // 2), HALF // 2)
-                    mine = s["q"][slot, :, place(sign * (NEAR + e)), side]
-                    s["raw_send"][g][side][rows, :] = mine.reshape(HALF // 2, HALF)
-                    raw[g, e, side, slot] = send(
-                        s["raw_send"][g][side].at[rows], s["raw"][g][side].at[rows], along_z(sign * e)
-                    )
+        for side in range(2):
+            arrived(slot, side)
+            for e in range(FAR, 0, -1):
+                for g, sign in enumerate(SIGNS):
+                    if e <= far_count(sign, side):
+                        rows = pl.ds(e * HALF + slot * (HALF // 2), HALF // 2)
+                        mine = s["q"][slot, :, side, place(sign * (NEAR + e))]
+                        s["raw_send"][g][side][rows, :] = mine.reshape(HALF // 2, HALF)
+                        raw[g, e, side, slot] = send(
+                            s["raw_send"][g][side].at[rows],
+                            s["raw"][g][side].at[rows],
+                            along_z(sign * e),
+                        )
 
     early = far_in(0)
     for copy in near + early:
@@ -358,21 +366,18 @@
             s["sum_send"][g][h][side].at[ROWS[c]], s["sum"][g][h][side].at[ROWS[c]], along_z(SIGNS[g])
         )
 
-    for n in range(2):
+    for side in range(2):
         for g, sign in enumerate(SIGNS):
-            side = streams(sign)[n]
-            count = far_count(sign, side)
-            for e in range(count, 0, -1):
-                for slot in range(2):
+            for slot in range(2):
+                for e in range(far_count(sign, side), 0, -1):
                     raw[g, e, side, slot].wait_recv()
         for c, rows in enumerate(ROWS):
             for g, sign in enumerate(SIGNS):
-                side = streams(sign)[n]
                 depth = (far_count(sign, side) + 1) * HALF
                 total = dot(s["hot_far"][g][side][rows, :depth], s["raw"][g][side][0:depth, :])
                 s["sum_send"][g][NEAR - 1][side][rows, :] = total.astype(BF16)
-                if n == 1:
-                    leave([chain[g, NEAR - 1, streams(sign)[0], c]])
+                if side == 1:
+                    leave([chain[g, NEAR - 1, 0, c]])
                 pass_on(g, NEAR - 1, side, c)
     for slot in range(2):
         arrived(slot, 3)
@@ -381,18 +386,17 @@
     for side in range(2):
         s["grad"][side][...] = dot(s["hot"][side][...], own_picks(0, side))
     for h in range(NEAR - 1, 0, -1):
-        for n in range(2):
+        for side in range(2):
             for c, rows in enumerate(ROWS):
-                for g, sign in enumerate(SIGNS):
-                    side = streams(sign)[n]
+                for g in range(2):
                     chain[g, h, side, c].wait_recv()
                     total = s["sum"][g][h][side][rows, :].astype(F32)
                     total = total + s["add"][h - 1][side][rows, g * HALF : (g + 1) * HALF]
                     s["sum_send"][g][h - 1][side][rows, :] = total.astype(BF16)
                     pass_on(g, h - 1, side, c)
     swap = {}
-    for c, rows in enumerate(ROWS):
-        for side in range(2):
+    for side in range(2):
+        for c, rows in enumerate(ROWS):
             for g in range(2):
                 chain[g, 0, side, c].wait_recv()
             s["grad"][side][rows, :] = (
@@ -401,11 +405,11 @@
                 + s["sum"][1][0][side][rows, :].astype(F32)
             )
             swap[side, c] = send(s["grad"][side].at[rows], s["other"][side].at[rows], partner)
-    for side, out in enumerate((out_innov_left, out_innov_right)):
         innov = s["innov"][side][...]
+        out = (out_innov_left, out_innov_right)[side]
         out[...] = innov - step_size * (s["grad"][side][...] + shrink * innov)
-    for c, rows in enumerate(ROWS):
-        for side, out in enumerate((out_common_left, out_common_right)):
+    for side, out in enumerate((out_common_left, out_common_right)):
+        for c, rows in enumerate(ROWS):
             swap[side, c].wait_recv()
             out[rows, :] = s["common"][side][rows, :] - step_size * (
                 s["grad"][side][rows, :] + s["other"][side][rows, :]
@@ -464,8 +468,8 @@
         "hot": [shard()] * 2,
         "hot_far": hot_far,
         "wide": [pltpu.VMEM((2 * EXT, HALF), F32)] * 2,
-        "back": pltpu.VMEM((2, NY - 1) + exchange, BF16),
-        "q": pltpu.VMEM((2, NY) + exchange, BF16),
+        "back": pltpu.VMEM((2, NY - 1, 2, NZ, 16, HALF), BF16),
+        "q": pltpu.VMEM((2, NY, 2, NZ, 16, HALF), BF16),
         "raw_send": raw,
         "raw": raw,
         "sum_send": [[[shard()] * 2 for _ in range(NEAR)] for _ in range(2)],

time: 103 us -> 102 us (level)
    pallas_call x1, Pallas kernels: 100 us -> 98.9 us  [per_device(): pl.pallas_call(kernel, out_shape=[jax.ShapeDtypeStruct((2 * rows, HALF),...]
where the time goes in v4:
time: 102 us
  Pallas kernels  101 us (99%)
    pallas_call x1, Pallas kernels, per_device(): pl.pallas_call(kernel, out_shape=[jax.ShapeDtypeStruct((2 * rows, HALF),...  98.9 us

profile of v4, /device:TPU:1, one launch (start us, length us, event | category | flops | bytes accessed | tf_op | source)
XLA Modules:
  0.0 101.6 jit_solution(13647764253755156028)
XLA Ops:
  0.6 98.9 %shard_map.120 = (f32[512,128]{1,0:T(8,128)}, f32[512,128]{1,0:T(8,128)}, f32[512,128]{1,0:T(8,128)}, f32[512,128]{1,0:T(8,128)}) custom-call(s32[2,2,2,64]{3,2,1,0:T(2,128)} %bitcast.16, s32[2,2,64]{2,1,0:T(2,128)} %bitcast.19, bf16[1,1,2,512,1024]{4,3,2,1,0:T(8,128)(2,1)} %observed.1, bf16[256,256]{1,0:T(8,128)(2,1)} %bitcast.12, ...), custom_call_target="tpu_custom_call" | custom-call | tf_op jit(solution)/shard_map/pallas_call | solution.py:498
  99.6 2.0 %shard_map.121 = (f32[512,128]{1,0:T(8,128)}, f32[512,128]{1,0:T(8,128)}, f32[512,128]{1,0:T(8,128)}, f32[512,128]{1,0:T(8,128)}) custom-call(f32[512,128]{1,0:T(8,128)} %get-tuple-element.12.refs_0_, f32[512,128]{1,0:T(8,128)} %get-tuple-element.13.refs_1_, f32[512,128]{1,0:T(8,128)} %get-tuple-element.14.refs_2_, f32[512,128]{1,0:T(8,128)} %get-tuple-element.15.refs_3_), custom_call_target="tpu_custom_call" | custom-call | tf_op jit(solution)/shard_map/pallas_call | solution.py:518

commit v5 on v4

--- a/solution.py
+++ b/solution.py
@@ -101,7 +101,8 @@
 
     commons = (common_left, common_right)
     innovs = (innov_left, innov_right)
-    for side in range(2):
+
+    def prepare(side):
         for src, dst in ((commons[side], s["common"][side]), (innovs[side], s["innov"][side])):
             x = src[...].astype(F32)
             dst[pl.ds(0, NB * 8, 2), :] = x[:, :HALF]
@@ -109,6 +110,7 @@
         joined = (s["common"][side][...] + s["innov"][side][...]).astype(BF16)
         s["own"][side][...] = joined.reshape(NB, 16, HALF)
 
+    prepare(0)
     pl.semaphore_wait(barrier, len(peers))
 
     dense = {}
@@ -121,6 +123,7 @@
                 )
 
     first_hop(0)
+    prepare(1)
 
     def choose(bufs, o):
         for k in range(NY):
@@ -243,13 +246,10 @@
             stage_far(g, side, 1)
     load_obs.wait()
     order_tile(0)
+    order_masks(0)
     leave([picks[key] for key in picks if key[3] == 0])
     for side in range(2):
         send_far(side, 1)
-    order_masks(0)
-    order_tile(1)
-    order_masks(1)
-
     def far_in(slot):
         copies = []
         for e in range(FAR, 0, -1):
@@ -319,32 +319,33 @@
 
     raw = {}
 
-    def far_out(slot):
-        for side in range(2):
-            arrived(slot, side)
-            for e in range(FAR, 0, -1):
-                for g, sign in enumerate(SIGNS):
-                    if e <= far_count(sign, side):
-                        rows = pl.ds(e * HALF + slot * (HALF // 2), HALF // 2)
-                        mine = s["q"][slot, :, side, place(sign * (NEAR + e))]
-                        s["raw_send"][g][side][rows, :] = mine.reshape(HALF // 2, HALF)
-                        raw[g, e, side, slot] = send(
-                            s["raw_send"][g][side].at[rows],
-                            s["raw"][g][side].at[rows],
-                            along_z(sign * e),
-                        )
+    def far_out(slot, side):
+        arrived(slot, side)
+        for e in range(FAR, 0, -1):
+            for g, sign in enumerate(SIGNS):
+                if e <= far_count(sign, side):
+                    rows = pl.ds(e * HALF + slot * (HALF // 2), HALF // 2)
+                    mine = s["q"][slot, :, side, place(sign * (NEAR + e))]
+                    s["raw_send"][g][side][rows, :] = mine.reshape(HALF // 2, HALF)
+                    raw[g, e, side, slot] = send(
+                        s["raw_send"][g][side].at[rows], s["raw"][g][side].at[rows], along_z(sign * e)
+                    )
 
     early = far_in(0)
+    order_tile(1)
+    order_masks(1)
     for copy in near + early:
         copy.wait_recv()
     tile(0)
     build_own_hot()
+    far_out(0, 0)
     late = far_in(1)
-    far_out(0)
+    far_out(0, 1)
     for copy in late:
         copy.wait_recv()
     tile(1)
-    far_out(1)
+    far_out(1, 0)
+    far_out(1, 1)
     for g in range(2):
         build_far_hot(g)
     for slot in range(2):

time: 102 us -> 102 us (level)
  no operation moved by 1% of the time
where the time goes in v5:
time: 102 us
  Pallas kernels  102 us (100%)
    pallas_call x1, Pallas kernels, per_device(): pl.pallas_call(kernel, out_shape=[jax.ShapeDtypeStruct((2 * rows, HALF),...  99.6 us

profile of v5, /device:TPU:1, one launch (start us, length us, event | category | flops | bytes accessed | tf_op | source)
XLA Modules:
  0.0 102.2 jit_solution(13810990216414343014)
XLA Ops:
  0.6 99.6 %shard_map.120 = (f32[512,128]{1,0:T(8,128)}, f32[512,128]{1,0:T(8,128)}, f32[512,128]{1,0:T(8,128)}, f32[512,128]{1,0:T(8,128)}) custom-call(s32[2,2,2,64]{3,2,1,0:T(2,128)} %bitcast.16, s32[2,2,64]{2,1,0:T(2,128)} %bitcast.19, bf16[1,1,2,512,1024]{4,3,2,1,0:T(8,128)(2,1)} %observed.1, bf16[256,256]{1,0:T(8,128)(2,1)} %bitcast.12, ...), custom_call_target="tpu_custom_call" | custom-call | tf_op jit(solution)/shard_map/pallas_call | solution.py:499
  100.3 2.0 %shard_map.121 = (f32[512,128]{1,0:T(8,128)}, f32[512,128]{1,0:T(8,128)}, f32[512,128]{1,0:T(8,128)}, f32[512,128]{1,0:T(8,128)}) custom-call(f32[512,128]{1,0:T(8,128)} %get-tuple-element.12.refs_0_, f32[512,128]{1,0:T(8,128)} %get-tuple-element.13.refs_1_, f32[512,128]{1,0:T(8,128)} %get-tuple-element.14.refs_2_, f32[512,128]{1,0:T(8,128)} %get-tuple-element.15.refs_3_), custom_call_target="tpu_custom_call" | custom-call | tf_op jit(solution)/shard_map/pallas_call | solution.py:519

commit v6 on v4

--- a/solution.py
+++ b/solution.py
@@ -15,7 +15,7 @@
 EXT = 512
 NB = 32
 HALF = 128
-NEAR = 3
+NEAR = 2
 FAR = NZ // 2 - NEAR
 SIGNS = (1, -1)
 HALVES = (pl.ds(0, NB // 2), pl.ds(NB // 2, NB // 2))

time: 102 us -> 100 us (0.980)
  Pallas kernels: 101 us -> 99.6 us
    pallas_call x1, Pallas kernels: 98.9 us -> 97.6 us  [per_device(): pl.pallas_call(kernel, out_shape=[jax.ShapeDtypeStruct((2 * rows, HALF),...]
where the time goes in v6:
time: 100 us
  Pallas kernels  99.6 us (100%)
    pallas_call x1, Pallas kernels, per_device(): pl.pallas_call(kernel, out_shape=[jax.ShapeDtypeStruct((2 * rows, HALF),...  97.6 us

profile of v6, /device:TPU:1, one launch (start us, length us, event | category | flops | bytes accessed | tf_op | source)
XLA Modules:
  0.0 100.2 jit_solution(1589515194946343380)
XLA Ops:
  0.6 97.6 %shard_map.120 = (f32[512,128]{1,0:T(8,128)}, f32[512,128]{1,0:T(8,128)}, f32[512,128]{1,0:T(8,128)}, f32[512,128]{1,0:T(8,128)}) custom-call(s32[2,2,2,64]{3,2,1,0:T(2,128)} %bitcast.16, s32[2,2,64]{2,1,0:T(2,128)} %bitcast.19, bf16[1,1,2,512,1024]{4,3,2,1,0:T(8,128)(2,1)} %observed.1, bf16[256,256]{1,0:T(8,128)(2,1)} %bitcast.12, ...), custom_call_target="tpu_custom_call" | custom-call | tf_op jit(solution)/shard_map/pallas_call | solution.py:498
  98.3 2.0 %shard_map.121 = (f32[512,128]{1,0:T(8,128)}, f32[512,128]{1,0:T(8,128)}, f32[512,128]{1,0:T(8,128)}, f32[512,128]{1,0:T(8,128)}) custom-call(f32[512,128]{1,0:T(8,128)} %get-tuple-element.12.refs_0_, f32[512,128]{1,0:T(8,128)} %get-tuple-element.13.refs_1_, f32[512,128]{1,0:T(8,128)} %get-tuple-element.14.refs_2_, f32[512,128]{1,0:T(8,128)} %get-tuple-element.15.refs_3_), custom_call_target="tpu_custom_call" | custom-call | tf_op jit(solution)/shard_map/pallas_call | solution.py:518

commit v7 on v5

--- a/solution.py
+++ b/solution.py
@@ -15,7 +15,7 @@
 EXT = 512
 NB = 32
 HALF = 128
-NEAR = 3
+NEAR = 2
 FAR = NZ // 2 - NEAR
 SIGNS = (1, -1)
 HALVES = (pl.ds(0, NB // 2), pl.ds(NB // 2, NB // 2))

time: 102 us -> 101 us (level)
  Pallas kernels: 102 us -> 99.9 us
    pallas_call x1, Pallas kernels: 99.6 us -> 97.9 us  [per_device(): pl.pallas_call(kernel, out_shape=[jax.ShapeDtypeStruct((2 * rows, HALF),...]
where the time goes in v7:
time: 101 us; the launch traced here: 100 us
  Pallas kernels  99.9 us (99%)
    pallas_call x1, Pallas kernels, per_device(): pl.pallas_call(kernel, out_shape=[jax.ShapeDtypeStruct((2 * rows, HALF),...  97.9 us

profile of v7, /device:TPU:1, one launch (start us, length us, event | category | flops | bytes accessed | tf_op | source)
XLA Modules:
  0.0 100.5 jit_solution(4480094319711717160)
XLA Ops:
  0.6 97.9 %shard_map.120 = (f32[512,128]{1,0:T(8,128)}, f32[512,128]{1,0:T(8,128)}, f32[512,128]{1,0:T(8,128)}, f32[512,128]{1,0:T(8,128)}) custom-call(s32[2,2,2,64]{3,2,1,0:T(2,128)} %bitcast.16, s32[2,2,64]{2,1,0:T(2,128)} %bitcast.19, bf16[1,1,2,512,1024]{4,3,2,1,0:T(8,128)(2,1)} %observed.1, bf16[256,256]{1,0:T(8,128)(2,1)} %bitcast.12, ...), custom_call_target="tpu_custom_call" | custom-call | tf_op jit(solution)/shard_map/pallas_call | solution.py:499
  98.5 2.0 %shard_map.121 = (f32[512,128]{1,0:T(8,128)}, f32[512,128]{1,0:T(8,128)}, f32[512,128]{1,0:T(8,128)}, f32[512,128]{1,0:T(8,128)}) custom-call(f32[512,128]{1,0:T(8,128)} %get-tuple-element.12.refs_0_, f32[512,128]{1,0:T(8,128)} %get-tuple-element.13.refs_1_, f32[512,128]{1,0:T(8,128)} %get-tuple-element.14.refs_2_, f32[512,128]{1,0:T(8,128)} %get-tuple-element.15.refs_3_), custom_call_target="tpu_custom_call" | custom-call | tf_op jit(solution)/shard_map/pallas_call | solution.py:519
